TPU v7x, 512 devices: a whole 4x8x8 slice. The times are simulated.
512 devices in a mesh: ctx: 64 (over y, z), head: 8 (over x, core).
Axes of the slice: x: 4, y: 8, z: 8, core: 2. Of those that a mesh axis runs over, the one named last changes fastest.
Arguments:
- queries: bfloat16 [32768, 4096], P('ctx', 'head'), may hold values from -6 to 6
- key_vectors: bfloat16 [32768, 4096], P('ctx', 'head'), may hold values from -6 to 6
- value_vectors: bfloat16 [32768, 4096], P('ctx', 'head'), may hold values from -360 to 360
- out_gain: bfloat16 [4096], P('head'), may hold values from 0.099609375 to 1.8984375
- out_grad: bfloat16 [32768, 4096], P('ctx', 'head'), may hold values from -6 to 6
Outputs:
- normed: bfloat16 [32768, 4096], P('ctx', 'head')
- query_grad: bfloat16 [32768, 4096], P('ctx', 'head')
- key_grad: bfloat16 [32768, 4096], P('ctx', 'head')
- value_grad: bfloat16 [32768, 4096], P('ctx', 'head')
All inputs are finite; a program needn't handle non-finite values.
Results may differ from a plain program's by a relative error of at most 0.005.
Values sent between devices are 32-bit elements; how exact they have to be, the bound alone decides.
A program may use at most 128 MiB of HBM per device.

v0:
```python
import math

import jax
import jax.numpy as jnp
from jax import lax
from jax.sharding import PartitionSpec as P

HD = 128
HID = 4096


epsilon = 1e-05


def carried_in(value, axis, combine, identity, reverse):
    devices, place = (lax.axis_size(axis), lax.axis_index(axis))
    everything = lax.all_gather(value, axis)
    start = jnp.broadcast_to(jnp.asarray(identity, value.dtype), value.shape)

    def step(k, before):
        at = devices - 1 - k if reverse else k
        reached = at > place if reverse else at < place
        new = combine(before, everything[at])
        return jnp.where(reached, new, before)

    return lax.fori_loop(0, devices, step, start)


def add_states(earlier, later_state):
    return earlier + later_state


def shards(queries, key_vectors, value_vectors, out_gain, out_grad):
    score_scale = 1.0 / math.sqrt(HD)
    tokens_here = queries.shape[0]
    width_here = queries.shape[1]
    heads_here = width_here // HD
    query_rows = queries.reshape(tokens_here, heads_here, HD)
    key_rows = key_vectors.reshape(tokens_here, heads_here, HD)
    value_rows = value_vectors.reshape(tokens_here, heads_here, HD)
    causal = jnp.tril(jnp.ones((tokens_here, tokens_here), dtype=bool))
    local_state = jnp.einsum(
        "thd,the->hde", key_rows, value_rows, preferred_element_type=jnp.float32
    )
    prior = carried_in(local_state, "ctx", add_states, jnp.zeros_like(local_state), False)
    scores = (
        jnp.einsum("thd,shd->hts", query_rows, key_rows, preferred_element_type=jnp.float32)
        * score_scale
    )
    weights = jnp.where(causal, scores, 0.0).astype(jnp.bfloat16)
    inner = jnp.einsum("hts,she->the", weights, value_rows, preferred_element_type=jnp.float32)
    outer = (
        jnp.einsum(
            "thd,hde->the", query_rows.astype(jnp.float32), prior, precision=lax.Precision.HIGHEST
        )
        * score_scale
    )
    attended = inner + outer
    gain_full = out_gain.astype(jnp.float32).reshape(heads_here, HD)
    grad_in = gain_full * out_grad.reshape(tokens_here, heads_here, HD).astype(jnp.float32)
    squares, crossed = lax.psum(
        (jnp.sum(attended * attended, axis=(1, 2)), jnp.sum(grad_in * attended, axis=(1, 2))),
        "head",
    )
    inverse_rms = lax.rsqrt(squares / HID + epsilon)[:, None, None]
    mean_cross = (crossed / HID)[:, None, None]
    normed = (attended * inverse_rms * gain_full).astype(jnp.bfloat16)
    grad_out = (
        inverse_rms * grad_in - attended * (inverse_rms * inverse_rms * inverse_rms * mean_cross)
    ).astype(jnp.bfloat16)
    local_grad = jnp.einsum(
        "thd,the->hde", query_rows, grad_out, preferred_element_type=jnp.float32
    )
    later = carried_in(local_grad, "ctx", add_states, jnp.zeros_like(local_grad), True)
    dscores = (
        jnp.einsum("the,she->hts", grad_out, value_rows, preferred_element_type=jnp.float32)
        * score_scale
    )
    dweights = jnp.where(causal, dscores, 0.0).astype(jnp.bfloat16)
    query_grad = (
        jnp.einsum("hts,shd->thd", dweights, key_rows, preferred_element_type=jnp.float32)
        + jnp.einsum(
            "the,hde->thd", grad_out.astype(jnp.float32), prior, precision=lax.Precision.HIGHEST
        )
        * score_scale
    )
    key_grad = (
        jnp.einsum("hts,thd->shd", dweights, query_rows, preferred_element_type=jnp.float32)
        + jnp.einsum(
            "she,hde->shd", value_rows.astype(jnp.float32), later, precision=lax.Precision.HIGHEST
        )
        * score_scale
    )
    value_grad = (
        jnp.einsum("hts,the->she", weights, grad_out, preferred_element_type=jnp.float32)
        + jnp.einsum(
            "shd,hde->she", key_rows.astype(jnp.float32), later, precision=lax.Precision.HIGHEST
        )
        * score_scale
    )
    return (
        normed.reshape(tokens_here, width_here),
        query_grad.astype(jnp.bfloat16).reshape(tokens_here, width_here),
        key_grad.astype(jnp.bfloat16).reshape(tokens_here, width_here),
        value_grad.astype(jnp.bfloat16).reshape(tokens_here, width_here),
    )


def solution(mesh):
    in_specs = (P("ctx", "head"), P("ctx", "head"), P("ctx", "head"), P("head"), P("ctx", "head"))
    out_specs = (P("ctx", "head"), P("ctx", "head"), P("ctx", "head"), P("ctx", "head"))
    return jax.shard_map(shards, mesh=mesh, in_specs=in_specs, out_specs=out_specs, check_vma=False)
```

profile of v0, /device:TPU:1, one launch (start us, length us, event | category | flops | bytes accessed | tf_op | source)
XLA Modules:
  0.0 463.7 jit_solution(7679075210120061619)
XLA Ops:
  7.3 1.4 copy.100
  8.6 2.0 fusion.13
  11.9 1.3 copy-done.1
  13.3 1.8 convolution_bitcast_fusion.2
  15.1 142.1 %all-gather.5.cloned.1.call-done = f32[256,128,128]{2,1,0:T(8,128)} async-done(((f32[4,128,128]{2,1,0:T(8,128)}), f32[256,128,128]{2,1,0:T(8,128)}) %all-gather.5.cloned.1.call-update) | async-done | bytes 16777232 | tf_op jit(solution)/shard_map/all_gather | solution.py:17
  157.2 68.1 %while.30 = (s32[]{:T(128)}, f32[4,128,128]{2,1,0:T(8,128)S(1)}, s32[]{:T(128)}, f32[64,4,128,128]{3,2,1,0:T(8,128)}, s32[]{:T(128)}, /*index=5*/s32[]{:T(128)}) while((s32[]{:T(128)}, f32[4,128,128]{2,1,0:T(8,128)S(1)}, s32[]{:T(128)}, f32[64,4,128,128]{3,2,1,0:T(8,128)}, s32[]{:T(128)}, /*index=5*/s32[]{:T(128)}) %tuple.89), condition=%wide.region_1.2_spmd.clone, body=%wide.region_0.1_spmd.clone.sunk | while | flops 196612 | bytes 786533 | solution.py:26
  162.5 1.0 add_select_fusion.4
  164.6 1.0 add_select_fusion.4
  166.7 1.0 add_select_fusion.4
  168.9 1.0 add_select_fusion.4
  171.0 1.0 add_select_fusion.4
  173.1 1.0 add_select_fusion.4
  182.7 1.0 add_select_fusion.4
  184.8 1.0 add_select_fusion.4
  225.3 3.0 multiply_reduce_fusion
  228.3 12.4 %all-reduce = (f32[512]{0:T(512)S(1)}, f32[512]{0:T(512)S(1)}) all-reduce(f32[512]{0:T(512)S(1)} %get-tuple-element.238, f32[512]{0:T(512)S(1)} %get-tuple-element.237), channel_id=1, replica_groups=mesh['ctx'=64,'head'=8] {'head'}, use_global_device_ids=true, to_apply=%region_3.4 | all-reduce | flops 1024 | bytes 8192 | tf_op jit(solution)/shard_map/psum | solution.py:61
  240.7 2.3 subtract_convert_fusion
  247.0 2.6 fusion.7
  249.6 2.0 copy.50
  251.6 2.6 fusion.32
  254.8 127.4 %all-gather.7.cloned.1.call-done = f32[256,128,128]{2,1,0:T(8,128)} async-done(((f32[4,128,128]{2,1,0:T(8,128)}), f32[256,128,128]{2,1,0:T(8,128)}) %all-gather.7.cloned.1.call-update) | async-done | bytes 16777232 | tf_op jit(solution)/shard_map/all_gather | solution.py:17
  382.1 68.4 %while.31 = (s32[]{:T(128)}, f32[4,128,128]{2,1,0:T(8,128)S(1)}, s32[]{:T(128)}, f32[64,4,128,128]{3,2,1,0:T(8,128)}, s32[]{:T(128)}, /*index=5*/s32[]{:T(128)}, s32[]{:T(128)}, s32[]{:T(128)}) while((s32[]{:T(128)}, f32[4,128,128]{2,1,0:T(8,128)S(1)}, s32[]{:T(128)}, f32[64,4,128,128]{3,2,1,0:T(8,128)}, s32[]{:T(128)}, ...), condition=%wide.region_7.8_spmd.clone, body=%wide.region_6.7_spmd.clone.sunk | while | flops 196616 | bytes 786595 | solution.py:26
  450.5 2.7 fusion.9
  453.2 2.0 copy.52
  (168 shorter events, 132.1 us)
Async XLA Ops:
  7.2 3.9 copy-start
  7.2 3.9 copy-start.8
  7.2 3.6 copy-start.11
  7.2 3.9 copy-start.14
  7.2 150.0 %all-gather.5.cloned.1.call-start = ((), (), s32[]{:S(2)}) async-start(), calls=%async_computation | async-start | bytes 17039360 | tf_op jit(solution)/shard_map/all_gather | solution.py:17
  10.7 371.4 %all-gather.7.cloned.1.call-start = ((), (), s32[]{:S(2)}) async-start(), calls=%async_computation.1 | async-start | bytes 17039360 | tf_op jit(solution)/shard_map/all_gather | solution.py:17
  11.1 0.8 copy-start.12
  11.1 2.2 copy-start.6
  11.9 1.3 copy-start.1
  243.0 3.1 copy-start.5
  243.0 1.2 copy-start.10
  243.0 2.2 copy-start.13
  246.2 3.4 copy-start.3
  247.0 4.7 %copy-start.2 = (bf16[4,512,512]{2,1,0:T(8,128)(2,1)S(1)}, bf16[4,512,512]{2,1,0:T(8,128)(2,1)}, u32[]{:S(2)}) copy-start(bf16[4,512,512]{2,1,0:T(8,128)(2,1)} %copy-done.1) | copy-start | bytes 6291460
  251.6 2.6 copy-start.4
  254.8 195.8 %copy-start.9 = (bf16[512,512]{1,0:T(8,128)(2,1)S(1)}, bf16[512,512]{1,0:T(8,128)(2,1)}, u32[]{:S(2)}) copy-start(bf16[512,512]{1,0:T(8,128)(2,1)} %param.10) | copy-start | bytes 1572868
  450.5 4.8 %copy-start.7 = (bf16[512,512]{1,0:T(8,128)(2,1)S(1)}, bf16[512,512]{1,0:T(8,128)(2,1)}, u32[]{:S(2)}) copy-start(bf16[512,512]{1,0:T(8,128)(2,1)} %param.11) | copy-start | bytes 1572868
Sparse Core Ops, SparseCore 0:
  11.6 145.4 all-gather.4
  244.3 137.7 all-gather.6
where the time goes:
time: 468 us; the launch traced here: 464 us
  waiting for transfers between devices  270 us (58%)
  other arithmetic  136 us (29%)
  matrix products  18.6 us (4%)
  between operations  14.3 us (3%)
  blocking collectives  12.4 us (3%)
  local copies, waits for them, and re-layouts  9.96 us (2%)
    all_gather x2, waiting for transfers between devices, carried_in(): everything = lax.all_gather(value, axis)  269 us
    select_n x128, other arithmetic, step(): return jnp.where(reached, new, before)  133 us
    psum x1, blocking collectives, shards(): lax.psum((jnp.sum(attended * attended, axis=(1, 2)), jnp.sum(grad_in * at...  12.4 us
  transfers between devices with their start and end apart: 2, of which 2 were waited for; matrix products, arithmetic and copies ran while one was open for 3% of the time, Pallas kernels for 0%

commit v1 on v0

v1 whole, which is shorter than its diff:
```python
import functools
import math

import jax
import jax.numpy as jnp
from jax import lax
from jax.experimental import pallas as pl
from jax.experimental.pallas import tpu as pltpu
from jax.sharding import PartitionSpec as P

HD = 128
TOK = 512
HEADS_HERE = 4
NZ = 8
EPSILON = 1e-05
SCALE = 1.0 / math.sqrt(HD)
MESH = pl.DeviceIdType.MESH
F32 = jnp.float32
BF16 = jnp.bfloat16


def product(a, b, contract):
    return lax.dot_general(a, b, ((contract[:1], contract[1:]), ((), ())), preferred_element_type=F32)


def rows_by_rows(a, b):
    return product(a, b, (1, 1))


def plain(a, b):
    return product(a, b, (1, 0))


def two_terms(state):
    high = state.astype(BF16)
    return high, (state - high.astype(F32)).astype(BF16)


def by_state(rows, state):
    high, low = two_terms(state)
    return plain(jnp.concatenate([rows, rows], axis=1), jnp.concatenate([high, low], axis=0)) * SCALE


def by_state_transposed(rows, state):
    high, low = two_terms(state)
    return rows_by_rows(jnp.concatenate([rows, rows], axis=1), jnp.concatenate([high, low], axis=1)) * SCALE


def score_block(a, b, keep):
    scores = rows_by_rows(a, b) * SCALE
    if keep is not None:
        scores = jnp.where(keep, scores, 0.0)
    return scores.astype(BF16)


def half_masks():
    half = TOK // 2
    rows = lax.broadcasted_iota(jnp.int32, (half, half), 0)
    columns = lax.broadcasted_iota(jnp.int32, (half, half), 1)
    return rows >= columns, rows <= columns


def sum_before(a, b, c, keep):
    half = TOK // 2
    first = plain(score_block(a[:half], b[:half], keep), c[:half])
    weights = jnp.concatenate([score_block(a[half:], b[:half], None), score_block(a[half:], b[half:], keep)], axis=1)
    return jnp.concatenate([first, plain(weights, c)], axis=0)


def sum_after(a, b, c, keep):
    half = TOK // 2
    weights = jnp.concatenate([score_block(a[:half], b[:half], keep), score_block(a[:half], b[half:], None)], axis=1)
    last = plain(score_block(a[half:], b[half:], keep), c[half:])
    return jnp.concatenate([plain(weights, c), last], axis=0)


def each_head(body):
    lax.fori_loop(0, HEADS_HERE, lambda h, _: (body(h), 0)[1], 0)


def attention_kernel(
    n_y, n_head,
    q_hbm, k_hbm, v_hbm, g_hbm, gain_ref,
    normed_ref, query_grad_ref, key_grad_ref, value_grad_ref,
    q, k, v, g, attended, inner_key, inner_value, do, prior, later,
    own, parts, totals, prefixes, total_out, sums, sums_out,
    in_sem, send_sem, recv_sem, sums_send, sums_recv,
):
    place, lane = lax.axis_index("ctx"), lax.axis_index("head")
    y, z = place // NZ, lax.rem(place, NZ)

    def along_z(other):
        return (y * NZ + other, lane)

    def along_y(other):
        return (other * NZ + z, lane)

    def along_head(other):
        return (place, other)

    def others(me, count):
        middle = count // 2
        steps = sorted(range(1, count), key=lambda step: (abs(step - middle), step))
        return [lax.rem(me + step, count) for step in steps]

    barrier = pltpu.get_barrier_semaphore()
    for me, count, device in ((z, NZ, along_z), (y, n_y, along_y), (lane, n_head, along_head)):
        for other in others(me, count):
            pl.semaphore_signal(barrier, inc=1, device_id=device(other), device_id_type=MESH)

    loads = []
    for source, target in ((k_hbm, k), (v_hbm, v), (q_hbm, q), (g_hbm, g)):
        loads.append([
            pltpu.make_async_copy(
                source.at[:, pl.ds(h * HD, HD)], target.at[h], in_sem.at[len(loads), h]
            )
            for h in range(HEADS_HERE)
        ])
    for pair in ((0, 1), (2, 3)):
        for h in range(HEADS_HERE):
            for which in pair:
                loads[which][h].start()

    def wait_all(phase, h, buffer, count):
        whole = buffer.at[h, pl.ds(0, count)]
        pltpu.make_async_remote_copy(
            src_ref=whole, dst_ref=whole, send_sem=send_sem.at[phase, h], recv_sem=recv_sem.at[phase, h],
            device_id=(place, lane), device_id_type=MESH,
        ).wait_recv()

    def wait_sent(phase, h, buffer, count):
        whole = buffer.at[h, pl.ds(0, count)]
        pltpu.make_async_remote_copy(
            src_ref=whole, dst_ref=whole, send_sem=send_sem.at[phase, h], recv_sem=recv_sem.at[phase, h],
            device_id=(place, lane), device_id_type=MESH,
        ).wait_send()

    def give_parts(scan, h):
        for other in others(z, NZ):
            pltpu.make_async_remote_copy(
                src_ref=own.at[scan, h, other], dst_ref=parts.at[scan, h, z],
                send_sem=send_sem.at[3 * scan, h], recv_sem=recv_sem.at[3 * scan, h],
                device_id=along_z(other), device_id_type=MESH,
            ).start()
        parts[scan, h, z] = own[scan, h, z]

    def give_totals(scan, h):
        wait_all(3 * scan, h, parts.at[scan], NZ - 1)
        running = jnp.zeros(parts.shape[3:], F32)
        for at in range(NZ) if scan == 0 else reversed(range(NZ)):
            prefixes[scan, h, at] = running
            running = running + parts[scan, h, at]
        total_out[scan, h] = running
        for other in others(y, n_y):
            pltpu.make_async_remote_copy(
                src_ref=total_out.at[scan, h], dst_ref=totals.at[scan, h, y],
                send_sem=send_sem.at[3 * scan + 1, h], recv_sem=recv_sem.at[3 * scan + 1, h],
                device_id=along_y(other), device_id_type=MESH,
            ).start()
        totals[scan, h, y] = running

    def give_prefixes(scan, h, state):
        wait_all(3 * scan + 1, h, totals.at[scan], n_y - 1)
        offset = jnp.zeros(parts.shape[3:], F32)
        for at in range(n_y) if scan == 0 else reversed(range(n_y)):
            reached = at < y if scan == 0 else at > y
            offset = jnp.where(reached, offset + totals[scan, h, at], offset)
        for at in range(NZ):
            prefixes[scan, h, at] = prefixes[scan, h, at] + offset
        for other in others(z, NZ):
            pltpu.make_async_remote_copy(
                src_ref=prefixes.at[scan, h, other], dst_ref=state.at[h, z],
                send_sem=send_sem.at[3 * scan + 2, h], recv_sem=recv_sem.at[3 * scan + 2, h],
                device_id=along_z(other), device_id_type=MESH,
            ).start()
        state[h, z] = prefixes[scan, h, z]

    def whole_state(scan, h, state):
        wait_all(3 * scan + 2, h, state, NZ - 1)
        return state[h].reshape(HD, HD)

    below, above = half_masks()

    for h in range(HEADS_HERE):
        loads[0][h].wait()
        loads[1][h].wait()
        own[0, h] = product(k[h], v[h], (0, 0)).reshape(own.shape[2:])
        if h == 0:
            pl.semaphore_wait(barrier, NZ + n_y + n_head - 3)
        give_parts(0, h)

    for h in range(HEADS_HERE):
        loads[2][h].wait()
        loads[3][h].wait()

    def inner_products(h):
        attended[h] = sum_before(q[h], k[h], v[h], below)

    each_head(inner_products)
    for h in range(HEADS_HERE):
        give_totals(0, h)
    for h in range(HEADS_HERE):
        give_prefixes(0, h, prior)

    squares = jnp.zeros((TOK, HD), F32)
    crossed = jnp.zeros((TOK, HD), F32)
    gains = [gain_ref[:, pl.ds(h * HD, HD)].astype(F32) for h in range(HEADS_HERE)]
    for h in range(HEADS_HERE):
        rows = attended[h] + by_state(q[h], whole_state(0, h, prior))
        attended[h] = rows
        squares = squares + rows * rows
        crossed = crossed + gains[h] * g[h].astype(F32) * rows

    ones = jnp.ones((8, HD), F32)
    row = lax.broadcasted_iota(jnp.int32, (8, HD), 0)
    packed = jnp.zeros((8, HD), F32)
    for first, array in ((0, squares), (4, crossed)):
        by_token = lax.dot_general(
            ones, array, (((1,), (1,)), ((), ())), precision=lax.Precision.HIGHEST, preferred_element_type=F32
        )
        for r in range(4):
            packed = jnp.where(row == first + r, by_token[:, r * HD : (r + 1) * HD], packed)
    sums_out[...] = packed
    for other in others(lane, n_head):
        pltpu.make_async_remote_copy(
            src_ref=sums_out, dst_ref=sums.at[lane], send_sem=sums_send, recv_sem=sums_recv,
            device_id=along_head(other), device_id_type=MESH,
        ).start()
    sums[lane] = packed
    arrived = sums.at[pl.ds(0, n_head - 1)]
    sums_wait = pltpu.make_async_remote_copy(
        src_ref=arrived, dst_ref=arrived, send_sem=sums_send, recv_sem=sums_recv,
        device_id=(place, lane), device_id_type=MESH,
    )
    sums_wait.wait_recv()
    total = sums[0]
    for at in range(1, n_head):
        total = total + sums[at]
    mean = total * (1.0 / (n_head * HEADS_HERE * HD))
    inverse_rms = lax.rsqrt(mean + EPSILON)
    cubed = inverse_rms * inverse_rms * inverse_rms
    cross_factor = pltpu.roll(cubed, 4, 0) * mean
    factors = jnp.where(row < 4, inverse_rms, cross_factor)
    columns = jnp.concatenate([factors] * (HD // 8), axis=0).T
    rms_column = jnp.concatenate([columns[:, r : r + 1] for r in range(4)], axis=0)
    cross_column = jnp.concatenate([columns[:, 4 + r : 5 + r] for r in range(4)], axis=0)

    for h in range(HEADS_HERE):
        grad_in = gains[h] * g[h].astype(F32)
        do[h] = (rms_column * grad_in - attended[h] * cross_column).astype(BF16)
        own[1, h] = product(q[h], do[h], (0, 0)).reshape(own.shape[2:])
        give_parts(1, h)

    for h in range(HEADS_HERE):
        normed_ref[h] = (attended[h] * rms_column * gains[h]).astype(BF16)

    def query_products(h):
        inner = sum_before(do[h], v[h], k[h], below)
        query_grad_ref[h] = (inner + by_state_transposed(do[h], prior[h].reshape(HD, HD))).astype(BF16)

    each_head(query_products)
    for h in range(HEADS_HERE):
        give_totals(1, h)

    def key_products(h):
        inner_key[h] = sum_after(v[h], do[h], q[h], above)
        inner_value[h] = sum_after(k[h], q[h], do[h], above)

    each_head(key_products)
    for h in range(HEADS_HERE):
        give_prefixes(1, h, later)
    for h in range(HEADS_HERE):
        state = whole_state(1, h, later)
        key_grad_ref[h] = (inner_key[h] + by_state_transposed(v[h], state)).astype(BF16)
        value_grad_ref[h] = (inner_value[h] + by_state(k[h], state)).astype(BF16)

    sums_wait.wait_send()
    for scan in range(2):
        for h in range(HEADS_HERE):
            wait_sent(3 * scan, h, parts.at[scan], NZ - 1)
            wait_sent(3 * scan + 1, h, totals.at[scan], n_y - 1)
            wait_sent(3 * scan + 2, h, prior, NZ - 1)


def store_kernel(*refs):
    sources, targets, sem = refs[:4], refs[4:8], refs[8]
    copies = [
        pltpu.make_async_copy(source.at[h], target.at[:, pl.ds(h * HD, HD)], sem.at[i, h])
        for i, (source, target) in enumerate(zip(sources, targets))
        for h in range(HEADS_HERE)
    ]
    for copy in copies:
        copy.start()
    for copy in copies:
        copy.wait()


def shards(n_y, n_head, queries, key_vectors, value_vectors, out_gain, out_grad):
    part = HD // NZ
    by_head = (HEADS_HERE, TOK, HD)
    state = (HEADS_HERE, NZ, part, HD)
    anywhere = pl.BlockSpec(memory_space=pl.ANY)
    vmem = pl.BlockSpec(memory_space=pltpu.VMEM)
    results = pl.pallas_call(
        functools.partial(attention_kernel, n_y, n_head),
        out_shape=[pltpu.VMEM(by_head, BF16)] * 4,
        in_specs=[anywhere] * 4 + [vmem],
        out_specs=[vmem] * 4,
        scratch_shapes=[pltpu.VMEM(by_head, BF16)] * 4
        + [pltpu.VMEM(by_head, F32)] * 3
        + [
            pltpu.VMEM(by_head, BF16),
            pltpu.VMEM(state, F32),
            pltpu.VMEM(state, F32),
            pltpu.VMEM((2,) + state, F32),
            pltpu.VMEM((2,) + state, F32),
            pltpu.VMEM((2, HEADS_HERE, n_y, part, HD), F32),
            pltpu.VMEM((2,) + state, F32),
            pltpu.VMEM((2, HEADS_HERE, part, HD), F32),
            pltpu.VMEM((n_head, 8, HD), F32),
            pltpu.VMEM((8, HD), F32),
            pltpu.SemaphoreType.DMA((4, HEADS_HERE)),
            pltpu.SemaphoreType.DMA((6, HEADS_HERE)),
            pltpu.SemaphoreType.DMA((6, HEADS_HERE)),
            pltpu.SemaphoreType.DMA,
            pltpu.SemaphoreType.DMA,
        ],
        compiler_params=pltpu.CompilerParams(
            collective_id=0, has_side_effects=True, vmem_limit_bytes=32 * 2**20
        ),
        name="attention",
    )(queries, key_vectors, value_vectors, out_grad, out_gain.reshape(1, HEADS_HERE * HD))
    whole = jax.ShapeDtypeStruct((TOK, HEADS_HERE * HD), BF16)
    return pl.pallas_call(
        store_kernel,
        out_shape=[whole] * 4,
        in_specs=[vmem] * 4,
        out_specs=[anywhere] * 4,
        scratch_shapes=[pltpu.SemaphoreType.DMA((4, HEADS_HERE))],
        name="store",
    )(*results)


def solution(mesh):
    n_y, n_head = mesh.shape["ctx"] // NZ, mesh.shape["head"]
    spec = P("ctx", "head")
    return jax.shard_map(
        functools.partial(shards, n_y, n_head),
        mesh=mesh,
        in_specs=(spec, spec, spec, P("head"), spec),
        out_specs=(spec,) * 4,
        check_vma=False,
    )
```

time: 468 us -> 69.3 us (0.15)
  waiting for transfers between devices: 270 us -> 0 us
  other arithmetic: 136 us -> 0 us
  Pallas kernels: 0 us -> 60.1 us
  matrix products: 18.6 us -> 0 us
  between operations: 14.3 us -> 0.65 us
  blocking collectives: 12.4 us -> 0 us
    all_gather x2 -> x0, waiting for transfers between devices: 269 us -> none  [carried_in(): everything = lax.all_gather(value, axis)]
    select_n x128 -> x0, other arithmetic: 133 us -> none  [step(): return jnp.where(reached, new, before)]
    pallas_call x0 -> x2, Pallas kernels: none -> 60.1 us  [the longest x1 57.1 us: shards(): pl.pallas_call(functools.partial(attention_kernel, n_y, n_head), out_shap...]
    dot_general x12 -> x0, matrix products: 18.6 us -> none  [the longest x1 3 us: shards(): jnp.einsum('thd,hde->the', query_rows.astype(jnp.float32), prior, precisi...]
    psum x1 -> x0, blocking collectives: 12.4 us -> none  [shards(): lax.psum((jnp.sum(attended * attended, axis=(1, 2)), jnp.sum(grad_in * at...]
  transfers between devices with their start and end apart: 2 -> 0, of which waited for: 2 -> 0; matrix products, arithmetic and copies ran while one was open for 3% -> 0% of each run, Pallas kernels for 0% -> 0%
where the time goes in v1:
time: 69.3 us; the launch traced here: 68.7 us
  Pallas kernels  60.1 us (87%)
  local copies, waits for them, and re-layouts  8.04 us (12%)
    pallas_call x1, Pallas kernels, shards(): pl.pallas_call(functools.partial(attention_kernel, n_y, n_head), out_shap...  57.1 us
    unnamed x16, local copies, waits for them, and re-layouts  7.36 us
    pallas_call x1, Pallas kernels, shards(): pl.pallas_call(store_kernel, out_shape=[whole] * 4, in_specs=[vmem] * 4,...  2.95 us

profile of v1, /device:TPU:1, one launch (start us, length us, event | category | flops | bytes accessed | tf_op | source)
XLA Modules:
  0.0 68.7 jit_solution(4392683300280271491)
XLA Ops:
  0.6 0.7 reshape.11.gain_ref
  1.3 0.0 copy-start
  1.3 1.0 %copy-done = bf16[512,512]{1,0:T(8,128)(2,1)S(1)} copy-done((bf16[512,512]{1,0:T(8,128)(2,1)S(1)}, bf16[512,512]{1,0:T(8,128)(2,1)}, u32[]{:S(2)}) %copy-start) | copy-done | bytes 524312
  2.4 0.0 copy-start.1
  2.4 1.0 %copy-done.1 = bf16[512,512]{1,0:T(8,128)(2,1)S(1)} copy-done((bf16[512,512]{1,0:T(8,128)(2,1)S(1)}, bf16[512,512]{1,0:T(8,128)(2,1)}, u32[]{:S(2)}) %copy-start.1) | copy-done | bytes 524312
  3.4 0.0 copy-start.2
  3.4 1.0 %copy-done.2 = bf16[512,512]{1,0:T(8,128)(2,1)S(1)} copy-done((bf16[512,512]{1,0:T(8,128)(2,1)S(1)}, bf16[512,512]{1,0:T(8,128)(2,1)}, u32[]{:S(2)}) %copy-start.2) | copy-done | bytes 524312
  4.4 0.0 copy-start.3
  4.4 1.0 %copy-done.3 = bf16[512,512]{1,0:T(8,128)(2,1)S(1)} copy-done((bf16[512,512]{1,0:T(8,128)(2,1)S(1)}, bf16[512,512]{1,0:T(8,128)(2,1)}, u32[]{:S(2)}) %copy-start.3) | copy-done | bytes 524312
  5.5 57.1 %attention.1 = (bf16[4,512,128]{2,1,0:T(8,128)(2,1)S(1)}, bf16[4,512,128]{2,1,0:T(8,128)(2,1)S(1)}, bf16[4,512,128]{2,1,0:T(8,128)(2,1)S(1)}, bf16[4,512,128]{2,1,0:T(8,128)(2,1)S(1)}) custom-call(bf16[512,512]{1,0:T(8,128)(2,1)S(1)} %copy-done, bf16[512,512]{1,0:T(8,128)(2,1)S(1)} %copy-done.1, bf16[512,512]{1,0:T(8,128)(2,1)S(1)} %copy-done.2, ...), custom_call_target="tpu_custom_call" | custom-call | tf_op jit(solution)/shard_map/attention/pallas_call | solution.py:304
  62.6 0.0 copy-start.4
  62.6 0.8 %copy-done.4 = bf16[4,512,128]{2,1,0:T(8,128)(2,1)} copy-done((bf16[4,512,128]{2,1,0:T(8,128)(2,1)}, bf16[4,512,128]{2,1,0:T(8,128)(2,1)S(1)}, u32[]{:S(2)}) %copy-start.4) | copy-done | bytes 524312
  63.4 0.0 copy-start.5
  63.4 0.8 %copy-done.5 = bf16[4,512,128]{2,1,0:T(8,128)(2,1)} copy-done((bf16[4,512,128]{2,1,0:T(8,128)(2,1)}, bf16[4,512,128]{2,1,0:T(8,128)(2,1)S(1)}, u32[]{:S(2)}) %copy-start.5) | copy-done | bytes 524312
  64.2 0.0 copy-start.6
  64.2 0.8 %copy-done.6 = bf16[4,512,128]{2,1,0:T(8,128)(2,1)} copy-done((bf16[4,512,128]{2,1,0:T(8,128)(2,1)}, bf16[4,512,128]{2,1,0:T(8,128)(2,1)S(1)}, u32[]{:S(2)}) %copy-start.6) | copy-done | bytes 524312
  65.0 0.0 copy-start.7
  65.0 0.8 %copy-done.7 = bf16[4,512,128]{2,1,0:T(8,128)(2,1)} copy-done((bf16[4,512,128]{2,1,0:T(8,128)(2,1)}, bf16[4,512,128]{2,1,0:T(8,128)(2,1)S(1)}, u32[]{:S(2)}) %copy-start.7) | copy-done | bytes 524312
  65.8 3.0 %store.1 = (bf16[512,512]{1,0:T(8,128)(2,1)}, bf16[512,512]{1,0:T(8,128)(2,1)}, bf16[512,512]{1,0:T(8,128)(2,1)}, bf16[512,512]{1,0:T(8,128)(2,1)}) custom-call(bf16[4,512,128]{2,1,0:T(8,128)(2,1)} %copy-done.4, bf16[4,512,128]{2,1,0:T(8,128)(2,1)} %copy-done.5, bf16[4,512,128]{2,1,0:T(8,128)(2,1)} %copy-done.6, bf16[4,512,128]{2,1,0:T(8,128)(2,1)} %copy-done.7), custom_call_target="tpu_custom_call" | custom-call | tf_op jit(solution)/shard_map/store/pallas_call | solution.py:334
Async XLA Ops:
  1.3 1.0 %copy-start = (bf16[512,512]{1,0:T(8,128)(2,1)S(1)}, bf16[512,512]{1,0:T(8,128)(2,1)}, u32[]{:S(2)}) copy-start(bf16[512,512]{1,0:T(8,128)(2,1)} %q_hbm.1) | copy-start | bytes 1572868
  2.4 1.0 %copy-start.1 = (bf16[512,512]{1,0:T(8,128)(2,1)S(1)}, bf16[512,512]{1,0:T(8,128)(2,1)}, u32[]{:S(2)}) copy-start(bf16[512,512]{1,0:T(8,128)(2,1)} %k_hbm.1) | copy-start | bytes 1572868
  3.4 1.0 %copy-start.2 = (bf16[512,512]{1,0:T(8,128)(2,1)S(1)}, bf16[512,512]{1,0:T(8,128)(2,1)}, u32[]{:S(2)}) copy-start(bf16[512,512]{1,0:T(8,128)(2,1)} %v_hbm.1) | copy-start | bytes 1572868
  4.4 1.0 %copy-start.3 = (bf16[512,512]{1,0:T(8,128)(2,1)S(1)}, bf16[512,512]{1,0:T(8,128)(2,1)}, u32[]{:S(2)}) copy-start(bf16[512,512]{1,0:T(8,128)(2,1)} %g_hbm.1) | copy-start | bytes 1572868
  62.6 0.8 %copy-start.4 = (bf16[4,512,128]{2,1,0:T(8,128)(2,1)}, bf16[4,512,128]{2,1,0:T(8,128)(2,1)S(1)}, u32[]{:S(2)}) copy-start(bf16[4,512,128]{2,1,0:T(8,128)(2,1)S(1)} %get-tuple-element.8.refs_0_) | copy-start | bytes 1572868
  63.4 0.8 %copy-start.5 = (bf16[4,512,128]{2,1,0:T(8,128)(2,1)}, bf16[4,512,128]{2,1,0:T(8,128)(2,1)S(1)}, u32[]{:S(2)}) copy-start(bf16[4,512,128]{2,1,0:T(8,128)(2,1)S(1)} %get-tuple-element.9.refs_1_) | copy-start | bytes 1572868
  64.2 0.8 %copy-start.6 = (bf16[4,512,128]{2,1,0:T(8,128)(2,1)}, bf16[4,512,128]{2,1,0:T(8,128)(2,1)S(1)}, u32[]{:S(2)}) copy-start(bf16[4,512,128]{2,1,0:T(8,128)(2,1)S(1)} %get-tuple-element.10.refs_2_) | copy-start | bytes 1572868
  65.0 0.8 %copy-start.7 = (bf16[4,512,128]{2,1,0:T(8,128)(2,1)}, bf16[4,512,128]{2,1,0:T(8,128)(2,1)S(1)}, u32[]{:S(2)}) copy-start(bf16[4,512,128]{2,1,0:T(8,128)(2,1)S(1)} %get-tuple-element.11.refs_3_) | copy-start | bytes 1572868

commit v2 on v1

--- a/solution.py
+++ b/solution.py
@@ -74,17 +74,21 @@
     return jnp.concatenate([plain(weights, c), last], axis=0)
 
 
+def columns_of(h):
+    return pl.ds(h * HD if isinstance(h, int) else pl.multiple_of(h * HD, HD), HD)
+
+
 def each_head(body):
     lax.fori_loop(0, HEADS_HERE, lambda h, _: (body(h), 0)[1], 0)
 
 
 def attention_kernel(
     n_y, n_head,
-    q_hbm, k_hbm, v_hbm, g_hbm, gain_ref,
+    q_hbm, k_hbm, v_hbm, g_hbm, gain_hbm,
     normed_ref, query_grad_ref, key_grad_ref, value_grad_ref,
-    q, k, v, g, attended, inner_key, inner_value, do, prior, later,
+    q, k, v, g, gain, attended, inner_key, inner_value, do, prior, later,
     own, parts, totals, prefixes, total_out, sums, sums_out,
-    in_sem, send_sem, recv_sem, sums_send, sums_recv,
+    in_sem, gain_sem, send_sem, recv_sem, sums_send, sums_recv,
 ):
     place, lane = lax.axis_index("ctx"), lax.axis_index("head")
     y, z = place // NZ, lax.rem(place, NZ)
@@ -116,10 +120,12 @@
             )
             for h in range(HEADS_HERE)
         ])
+    gain_load = pltpu.make_async_copy(gain_hbm, gain, gain_sem)
     for pair in ((0, 1), (2, 3)):
         for h in range(HEADS_HERE):
             for which in pair:
                 loads[which][h].start()
+    gain_load.start()
 
     def wait_all(phase, h, buffer, count):
         whole = buffer.at[h, pl.ds(0, count)]
@@ -146,9 +152,9 @@
 
     def give_totals(scan, h):
         wait_all(3 * scan, h, parts.at[scan], NZ - 1)
-        running = jnp.zeros(parts.shape[3:], F32)
-        for at in range(NZ) if scan == 0 else reversed(range(NZ)):
-            prefixes[scan, h, at] = running
+        order = list(range(NZ)) if scan == 0 else list(reversed(range(NZ)))
+        running = parts[scan, h, order[0]]
+        for at in order[1:]:
             running = running + parts[scan, h, at]
         total_out[scan, h] = running
         for other in others(y, n_y):
@@ -158,6 +164,10 @@
                 device_id=along_y(other), device_id_type=MESH,
             ).start()
         totals[scan, h, y] = running
+        running = jnp.zeros(parts.shape[3:], F32)
+        for at in order:
+            prefixes[scan, h, at] = running
+            running = running + parts[scan, h, at]
 
     def give_prefixes(scan, h, state):
         wait_all(3 * scan + 1, h, totals.at[scan], n_y - 1)
@@ -167,7 +177,7 @@
             offset = jnp.where(reached, offset + totals[scan, h, at], offset)
         for at in range(NZ):
             prefixes[scan, h, at] = prefixes[scan, h, at] + offset
-        for other in others(z, NZ):
+        for other in others(z, NZ) if scan == 0 else others(z, NZ):
             pltpu.make_async_remote_copy(
                 src_ref=prefixes.at[scan, h, other], dst_ref=state.at[h, z],
                 send_sem=send_sem.at[3 * scan + 2, h], recv_sem=recv_sem.at[3 * scan + 2, h],
@@ -192,6 +202,7 @@
     for h in range(HEADS_HERE):
         loads[2][h].wait()
         loads[3][h].wait()
+    gain_load.wait()
 
     def inner_products(h):
         attended[h] = sum_before(q[h], k[h], v[h], below)
@@ -204,7 +215,7 @@
 
     squares = jnp.zeros((TOK, HD), F32)
     crossed = jnp.zeros((TOK, HD), F32)
-    gains = [gain_ref[:, pl.ds(h * HD, HD)].astype(F32) for h in range(HEADS_HERE)]
+    gains = [gain[pl.ds(h * HD, HD)].astype(F32).reshape(1, HD) for h in range(HEADS_HERE)]
     for h in range(HEADS_HERE):
         rows = attended[h] + by_state(q[h], whole_state(0, h, prior))
         attended[h] = rows
@@ -252,42 +263,45 @@
         give_parts(1, h)
 
     for h in range(HEADS_HERE):
-        normed_ref[h] = (attended[h] * rms_column * gains[h]).astype(BF16)
+        normed_ref[:, columns_of(h)] = (attended[h] * rms_column * gains[h]).astype(BF16)
 
     def query_products(h):
         inner = sum_before(do[h], v[h], k[h], below)
-        query_grad_ref[h] = (inner + by_state_transposed(do[h], prior[h].reshape(HD, HD))).astype(BF16)
+        query_grad_ref[:, columns_of(h)] = (inner + by_state_transposed(do[h], prior[h].reshape(HD, HD))).astype(BF16)
 
     each_head(query_products)
-    for h in range(HEADS_HERE):
-        give_totals(1, h)
 
     def key_products(h):
         inner_key[h] = sum_after(v[h], do[h], q[h], above)
         inner_value[h] = sum_after(k[h], q[h], do[h], above)
 
-    each_head(key_products)
-    for h in range(HEADS_HERE):
-        give_prefixes(1, h, later)
-    for h in range(HEADS_HERE):
-        state = whole_state(1, h, later)
-        key_grad_ref[h] = (inner_key[h] + by_state_transposed(v[h], state)).astype(BF16)
-        value_grad_ref[h] = (inner_value[h] + by_state(k[h], state)).astype(BF16)
-
-    sums_wait.wait_send()
+    for h in range(HEADS_HERE):
+        give_totals(1, h)
+        key_products(h)
     for scan in range(2):
         for h in range(HEADS_HERE):
             wait_sent(3 * scan, h, parts.at[scan], NZ - 1)
-            wait_sent(3 * scan + 1, h, totals.at[scan], n_y - 1)
-            wait_sent(3 * scan + 2, h, prior, NZ - 1)
+    for h in range(HEADS_HERE):
+        wait_sent(1, h, totals.at[0], n_y - 1)
+        wait_sent(2, h, prior, NZ - 1)
+    sums_wait.wait_send()
+    for h in range(HEADS_HERE):
+        give_prefixes(1, h, later)
+    for h in range(HEADS_HERE):
+        state = whole_state(1, h, later)
+        key_grad_ref[:, columns_of(h)] = (inner_key[h] + by_state_transposed(v[h], state)).astype(BF16)
+        value_grad_ref[:, columns_of(h)] = (inner_value[h] + by_state(k[h], state)).astype(BF16)
+
+    for h in range(HEADS_HERE):
+        wait_sent(4, h, totals.at[1], n_y - 1)
+        wait_sent(5, h, later, NZ - 1)
 
 
 def store_kernel(*refs):
     sources, targets, sem = refs[:4], refs[4:8], refs[8]
     copies = [
-        pltpu.make_async_copy(source.at[h], target.at[:, pl.ds(h * HD, HD)], sem.at[i, h])
+        pltpu.make_async_copy(source, target, sem.at[i])
         for i, (source, target) in enumerate(zip(sources, targets))
-        for h in range(HEADS_HERE)
     ]
     for copy in copies:
         copy.start()
@@ -303,10 +317,11 @@
     vmem = pl.BlockSpec(memory_space=pltpu.VMEM)
     results = pl.pallas_call(
         functools.partial(attention_kernel, n_y, n_head),
-        out_shape=[pltpu.VMEM(by_head, BF16)] * 4,
-        in_specs=[anywhere] * 4 + [vmem],
+        out_shape=[pltpu.VMEM((TOK, HEADS_HERE * HD), BF16)] * 4,
+        in_specs=[anywhere] * 5,
         out_specs=[vmem] * 4,
         scratch_shapes=[pltpu.VMEM(by_head, BF16)] * 4
+        + [pltpu.VMEM((HEADS_HERE * HD,), BF16)]
         + [pltpu.VMEM(by_head, F32)] * 3
         + [
             pltpu.VMEM(by_head, BF16),
@@ -320,23 +335,25 @@
             pltpu.VMEM((n_head, 8, HD), F32),
             pltpu.VMEM((8, HD), F32),
             pltpu.SemaphoreType.DMA((4, HEADS_HERE)),
+            pltpu.SemaphoreType.DMA,
             pltpu.SemaphoreType.DMA((6, HEADS_HERE)),
             pltpu.SemaphoreType.DMA((6, HEADS_HERE)),
             pltpu.SemaphoreType.DMA,
             pltpu.SemaphoreType.DMA,
         ],
         compiler_params=pltpu.CompilerParams(
-            collective_id=0, has_side_effects=True, vmem_limit_bytes=32 * 2**20
+            collective_id=0, has_side_effects=True, vmem_limit_bytes=56 * 2**20
         ),
         name="attention",
-    )(queries, key_vectors, value_vectors, out_grad, out_gain.reshape(1, HEADS_HERE * HD))
+    )(queries, key_vectors, value_vectors, out_grad, out_gain)
     whole = jax.ShapeDtypeStruct((TOK, HEADS_HERE * HD), BF16)
     return pl.pallas_call(
         store_kernel,
         out_shape=[whole] * 4,
-        in_specs=[vmem] * 4,
+        in_specs=[anywhere] * 4,
         out_specs=[anywhere] * 4,
-        scratch_shapes=[pltpu.SemaphoreType.DMA((4, HEADS_HERE))],
+        scratch_shapes=[pltpu.SemaphoreType.DMA((4,))],
+        compiler_params=pltpu.CompilerParams(vmem_limit_bytes=2**20),
         name="store",
     )(*results)
 

time: 69.3 us -> 57.8 us (0.83)
  local copies, waits for them, and re-layouts: 8.04 us -> 0 us
  Pallas kernels: 60.1 us -> 56.5 us
    unnamed x16 -> x0, local copies, waits for them, and re-layouts: 7.36 us -> none
    pallas_call x1, Pallas kernels: 57.1 us -> 55.1 us  [shards(): pl.pallas_call(functools.partial(attention_kernel, n_y, n_head), out_shap...]
    pallas_call x1, Pallas kernels: 2.95 us -> 1.35 us  [shards(): pl.pallas_call(store_kernel, out_shape=[whole] * 4, in_specs=[anywhere] *...]
where the time goes in v2:
time: 57.8 us; the launch traced here: 57.1 us
  Pallas kernels  56.5 us (98%)
  between operations  0.64 us (1%)
    pallas_call x1, Pallas kernels, shards(): pl.pallas_call(functools.partial(attention_kernel, n_y, n_head), out_shap...  55.1 us
    pallas_call x1, Pallas kernels, shards(): pl.pallas_call(store_kernel, out_shape=[whole] * 4, in_specs=[anywhere] *...  1.35 us

profile of v2, /device:TPU:1, one launch (start us, length us, event | category | flops | bytes accessed | tf_op | source)
XLA Modules:
  0.0 57.1 jit_solution(4650320634123544622)
XLA Ops:
  0.6 55.1 %attention.1 = (bf16[512,512]{1,0:T(8,128)(2,1)S(1)}, bf16[512,512]{1,0:T(8,128)(2,1)S(1)}, bf16[512,512]{1,0:T(8,128)(2,1)S(1)}, bf16[512,512]{1,0:T(8,128)(2,1)S(1)}) custom-call(bf16[512,512]{1,0:T(8,128)(2,1)} %q_hbm.1, bf16[512,512]{1,0:T(8,128)(2,1)} %k_hbm.1, bf16[512,512]{1,0:T(8,128)(2,1)} %v_hbm.1, bf16[512,512]{1,0:T(8,128)(2,1)} %g_hbm.1, ...), custom_call_target="tpu_custom_call" | custom-call | tf_op jit(solution)/shard_map/attention/pallas_call | solution.py:318
  55.8 1.3 %store.1 = (bf16[512,512]{1,0:T(8,128)(2,1)}, bf16[512,512]{1,0:T(8,128)(2,1)}, bf16[512,512]{1,0:T(8,128)(2,1)}, bf16[512,512]{1,0:T(8,128)(2,1)}) custom-call(bf16[512,512]{1,0:T(8,128)(2,1)S(1)} %get-tuple-element.8.refs_0_, bf16[512,512]{1,0:T(8,128)(2,1)S(1)} %get-tuple-element.9.refs_1_, bf16[512,512]{1,0:T(8,128)(2,1)S(1)} %get-tuple-element.10.refs_2_, ...), custom_call_target="tpu_custom_call" | custom-call | tf_op jit(solution)/shard_map/store/pallas_call | solution.py:350

commit v3 on v2

--- a/solution.py
+++ b/solution.py
@@ -12,6 +12,8 @@
 TOK = 512
 HEADS_HERE = 4
 NZ = 8
+SPLIT = 1
+GROUPS = HEADS_HERE * SPLIT
 EPSILON = 1e-05
 SCALE = 1.0 / math.sqrt(HD)
 MESH = pl.DeviceIdType.MESH
@@ -75,18 +77,18 @@
 
 
 def columns_of(h):
-    return pl.ds(h * HD if isinstance(h, int) else pl.multiple_of(h * HD, HD), HD)
-
-
-def each_head(body):
-    lax.fori_loop(0, HEADS_HERE, lambda h, _: (body(h), 0)[1], 0)
+    return pl.ds(pl.multiple_of(h * HD, HD), HD)
+
+
+def each(count, body):
+    lax.fori_loop(0, count, lambda i, _: (body(i), 0)[1], 0)
 
 
 def attention_kernel(
     n_y, n_head,
     q_hbm, k_hbm, v_hbm, g_hbm, gain_hbm,
     normed_ref, query_grad_ref, key_grad_ref, value_grad_ref,
-    q, k, v, g, gain, attended, inner_key, inner_value, do, prior, later,
+    q, k, v, g, gain, gain_rows, q_turned, grad_in, squares, crossed, attended, inner_key, inner_value, do, prior, later,
     own, parts, totals, prefixes, total_out, sums, sums_out,
     in_sem, gain_sem, send_sem, recv_sem, sums_send, sums_recv,
 ):
@@ -112,19 +114,22 @@
         for other in others(me, count):
             pl.semaphore_signal(barrier, inc=1, device_id=device(other), device_id_type=MESH)
 
-    loads = []
-    for source, target in ((k_hbm, k), (v_hbm, v), (q_hbm, q), (g_hbm, g)):
-        loads.append([
-            pltpu.make_async_copy(
-                source.at[:, pl.ds(h * HD, HD)], target.at[h], in_sem.at[len(loads), h]
-            )
-            for h in range(HEADS_HERE)
-        ])
+    def load(which, h):
+        source, target = ((k_hbm, k), (v_hbm, v), (q_hbm, q), (g_hbm, g))[which]
+        return pltpu.make_async_copy(source.at[:, columns_of(h)], target.at[h], in_sem.at[which, h])
+
     gain_load = pltpu.make_async_copy(gain_hbm, gain, gain_sem)
-    for pair in ((0, 1), (2, 3)):
-        for h in range(HEADS_HERE):
-            for which in pair:
-                loads[which][h].start()
+
+    @functools.partial(each, HEADS_HERE)
+    def load_keys(h):
+        load(0, h).start()
+        load(1, h).start()
+
+    @functools.partial(each, HEADS_HERE)
+    def load_queries(h):
+        load(2, h).start()
+        load(3, h).start()
+
     gain_load.start()
 
     def wait_all(phase, h, buffer, count):
@@ -186,49 +191,56 @@
         state[h, z] = prefixes[scan, h, z]
 
     def whole_state(scan, h, state):
-        wait_all(3 * scan + 2, h, state, NZ - 1)
-        return state[h].reshape(HD, HD)
+        for at in range(SPLIT):
+            wait_all(3 * scan + 2, h * SPLIT + at, state, NZ - 1)
+        return state[pl.ds(h * SPLIT, SPLIT)].reshape(HD, HD)
 
     below, above = half_masks()
 
+    @functools.partial(each, HEADS_HERE)
+    def key_value_state(h):
+        load(0, h).wait()
+        load(1, h).wait()
+        own[0, pl.ds(h * SPLIT, SPLIT)] = product(k[h], v[h], (0, 0)).reshape((SPLIT,) + own.shape[2:])
+
+    pl.semaphore_wait(barrier, NZ + n_y + n_head - 3)
+    each(GROUPS, functools.partial(give_parts, 0))
+
+    @functools.partial(each, HEADS_HERE)
+    def inner_products(h):
+        load(2, h).wait()
+        load(3, h).wait()
+        attended[h] = sum_before(q[h], k[h], v[h], below)
+
+    def gain_row(h):
+        return gain_rows[h]
+
+    gain_load.wait()
     for h in range(HEADS_HERE):
-        loads[0][h].wait()
-        loads[1][h].wait()
-        own[0, h] = product(k[h], v[h], (0, 0)).reshape(own.shape[2:])
-        if h == 0:
-            pl.semaphore_wait(barrier, NZ + n_y + n_head - 3)
-        give_parts(0, h)
-
-    for h in range(HEADS_HERE):
-        loads[2][h].wait()
-        loads[3][h].wait()
-    gain_load.wait()
-
-    def inner_products(h):
-        attended[h] = sum_before(q[h], k[h], v[h], below)
-
-    each_head(inner_products)
-    for h in range(HEADS_HERE):
-        give_totals(0, h)
-    for h in range(HEADS_HERE):
-        give_prefixes(0, h, prior)
-
-    squares = jnp.zeros((TOK, HD), F32)
-    crossed = jnp.zeros((TOK, HD), F32)
-    gains = [gain[pl.ds(h * HD, HD)].astype(F32).reshape(1, HD) for h in range(HEADS_HERE)]
-    for h in range(HEADS_HERE):
+        gain_rows[h] = gain[pl.ds(h * HD, HD)].astype(F32).reshape(1, HD)
+    squares[...] = jnp.zeros((TOK, HD), F32)
+    crossed[...] = jnp.zeros((TOK, HD), F32)
+
+    @functools.partial(each, HEADS_HERE)
+    def scaled_gradients(h):
+        q_turned[h] = q[h].T
+        grad_in[h] = gain_row(h) * g[h].astype(F32)
+
+    each(GROUPS, functools.partial(give_totals, 0))
+    each(GROUPS, lambda group: give_prefixes(0, group, prior))
+
+    @functools.partial(each, HEADS_HERE)
+    def outer_products(h):
         rows = attended[h] + by_state(q[h], whole_state(0, h, prior))
         attended[h] = rows
-        squares = squares + rows * rows
-        crossed = crossed + gains[h] * g[h].astype(F32) * rows
-
-    ones = jnp.ones((8, HD), F32)
+        squares[...] += rows * rows
+        crossed[...] += grad_in[h] * rows
+
+    ones = jnp.ones((8, 2 * HD), BF16)
     row = lax.broadcasted_iota(jnp.int32, (8, HD), 0)
     packed = jnp.zeros((8, HD), F32)
-    for first, array in ((0, squares), (4, crossed)):
-        by_token = lax.dot_general(
-            ones, array, (((1,), (1,)), ((), ())), precision=lax.Precision.HIGHEST, preferred_element_type=F32
-        )
+    for first, array in ((0, squares[...]), (4, crossed[...])):
+        by_token = rows_by_rows(ones, jnp.concatenate(two_terms(array), axis=1))
         for r in range(4):
             packed = jnp.where(row == first + r, by_token[:, r * HD : (r + 1) * HD], packed)
     sums_out[...] = packed
@@ -256,45 +268,48 @@
     rms_column = jnp.concatenate([columns[:, r : r + 1] for r in range(4)], axis=0)
     cross_column = jnp.concatenate([columns[:, 4 + r : 5 + r] for r in range(4)], axis=0)
 
-    for h in range(HEADS_HERE):
-        grad_in = gains[h] * g[h].astype(F32)
-        do[h] = (rms_column * grad_in - attended[h] * cross_column).astype(BF16)
-        own[1, h] = product(q[h], do[h], (0, 0)).reshape(own.shape[2:])
-        give_parts(1, h)
-
-    for h in range(HEADS_HERE):
-        normed_ref[:, columns_of(h)] = (attended[h] * rms_column * gains[h]).astype(BF16)
-
+    @functools.partial(each, HEADS_HERE)
+    def query_state(h):
+        do[h] = (rms_column * grad_in[h] - attended[h] * cross_column).astype(BF16)
+        own[1, pl.ds(h * SPLIT, SPLIT)] = plain(q_turned[h], do[h]).reshape((SPLIT,) + own.shape[2:])
+        for at in range(SPLIT):
+            give_parts(1, h * SPLIT + at)
+
+    @functools.partial(each, HEADS_HERE)
     def query_products(h):
+        normed_ref[:, columns_of(h)] = (attended[h] * rms_column * gain_row(h)).astype(BF16)
         inner = sum_before(do[h], v[h], k[h], below)
-        query_grad_ref[:, columns_of(h)] = (inner + by_state_transposed(do[h], prior[h].reshape(HD, HD))).astype(BF16)
-
-    each_head(query_products)
-
+        state = prior[pl.ds(h * SPLIT, SPLIT)].reshape(HD, HD)
+        query_grad_ref[:, columns_of(h)] = (inner + by_state_transposed(do[h], state)).astype(BF16)
+
+    @functools.partial(each, HEADS_HERE)
     def key_products(h):
+        for at in range(SPLIT):
+            give_totals(1, h * SPLIT + at)
         inner_key[h] = sum_after(v[h], do[h], q[h], above)
         inner_value[h] = sum_after(k[h], q[h], do[h], above)
 
-    for h in range(HEADS_HERE):
-        give_totals(1, h)
-        key_products(h)
-    for scan in range(2):
-        for h in range(HEADS_HERE):
-            wait_sent(3 * scan, h, parts.at[scan], NZ - 1)
-    for h in range(HEADS_HERE):
-        wait_sent(1, h, totals.at[0], n_y - 1)
-        wait_sent(2, h, prior, NZ - 1)
     sums_wait.wait_send()
-    for h in range(HEADS_HERE):
-        give_prefixes(1, h, later)
-    for h in range(HEADS_HERE):
+
+    @functools.partial(each, GROUPS)
+    def earlier_sends(group):
+        wait_sent(0, group, parts.at[0], NZ - 1)
+        wait_sent(1, group, totals.at[0], n_y - 1)
+        wait_sent(2, group, prior, NZ - 1)
+        wait_sent(3, group, parts.at[1], NZ - 1)
+
+    each(GROUPS, lambda group: give_prefixes(1, group, later))
+
+    @functools.partial(each, HEADS_HERE)
+    def key_and_value_grads(h):
         state = whole_state(1, h, later)
         key_grad_ref[:, columns_of(h)] = (inner_key[h] + by_state_transposed(v[h], state)).astype(BF16)
         value_grad_ref[:, columns_of(h)] = (inner_value[h] + by_state(k[h], state)).astype(BF16)
 
-    for h in range(HEADS_HERE):
-        wait_sent(4, h, totals.at[1], n_y - 1)
-        wait_sent(5, h, later, NZ - 1)
+    @functools.partial(each, GROUPS)
+    def last_sends(group):
+        wait_sent(4, group, totals.at[1], n_y - 1)
+        wait_sent(5, group, later, NZ - 1)
 
 
 def store_kernel(*refs):
@@ -310,9 +325,9 @@
 
 
 def shards(n_y, n_head, queries, key_vectors, value_vectors, out_gain, out_grad):
-    part = HD // NZ
+    part = HD // (NZ * SPLIT)
     by_head = (HEADS_HERE, TOK, HD)
-    state = (HEADS_HERE, NZ, part, HD)
+    state = (GROUPS, NZ, part, HD)
     anywhere = pl.BlockSpec(memory_space=pl.ANY)
     vmem = pl.BlockSpec(memory_space=pltpu.VMEM)
     results = pl.pallas_call(
@@ -321,7 +336,9 @@
         in_specs=[anywhere] * 5,
         out_specs=[vmem] * 4,
         scratch_shapes=[pltpu.VMEM(by_head, BF16)] * 4
-        + [pltpu.VMEM((HEADS_HERE * HD,), BF16)]
+        + [pltpu.VMEM((HEADS_HERE * HD,), BF16), pltpu.VMEM((HEADS_HERE, 1, HD), F32)]
+        + [pltpu.VMEM((HEADS_HERE, HD, TOK), BF16), pltpu.VMEM(by_head, F32)]
+        + [pltpu.VMEM((TOK, HD), F32)] * 2
         + [pltpu.VMEM(by_head, F32)] * 3
         + [
             pltpu.VMEM(by_head, BF16),
@@ -329,20 +346,20 @@
             pltpu.VMEM(state, F32),
             pltpu.VMEM((2,) + state, F32),
             pltpu.VMEM((2,) + state, F32),
-            pltpu.VMEM((2, HEADS_HERE, n_y, part, HD), F32),
+            pltpu.VMEM((2, GROUPS, n_y, part, HD), F32),
             pltpu.VMEM((2,) + state, F32),
-            pltpu.VMEM((2, HEADS_HERE, part, HD), F32),
+            pltpu.VMEM((2, GROUPS, part, HD), F32),
             pltpu.VMEM((n_head, 8, HD), F32),
             pltpu.VMEM((8, HD), F32),
             pltpu.SemaphoreType.DMA((4, HEADS_HERE)),
             pltpu.SemaphoreType.DMA,
-            pltpu.SemaphoreType.DMA((6, HEADS_HERE)),
-            pltpu.SemaphoreType.DMA((6, HEADS_HERE)),
+            pltpu.SemaphoreType.DMA((6, GROUPS)),
+            pltpu.SemaphoreType.DMA((6, GROUPS)),
             pltpu.SemaphoreType.DMA,
             pltpu.SemaphoreType.DMA,
         ],
         compiler_params=pltpu.CompilerParams(
-            collective_id=0, has_side_effects=True, vmem_limit_bytes=56 * 2**20
+            collective_id=0, has_side_effects=True, vmem_limit_bytes=58 * 2**20
         ),
         name="attention",
     )(queries, key_vectors, value_vectors, out_grad, out_gain)

time: 57.8 us -> 57.3 us (level)
  no operation moved by 1% of the time
where the time goes in v3:
time: 57.3 us; the launch traced here: 57.2 us
  Pallas kernels  56.5 us (99%)
  between operations  0.64 us (1%)
    pallas_call x1, Pallas kernels, shards(): pl.pallas_call(functools.partial(attention_kernel, n_y, n_head), out_shap...  55.2 us
    pallas_call x1, Pallas kernels, shards(): pl.pallas_call(store_kernel, out_shape=[whole] * 4, in_specs=[anywhere] *...  1.35 us

profile of v3, /device:TPU:1, one launch (start us, length us, event | category | flops | bytes accessed | tf_op | source)
XLA Modules:
  0.0 57.2 jit_solution(15890119680919972109)
XLA Ops:
  0.6 55.2 %attention.1 = (bf16[512,512]{1,0:T(8,128)(2,1)S(1)}, bf16[512,512]{1,0:T(8,128)(2,1)S(1)}, bf16[512,512]{1,0:T(8,128)(2,1)S(1)}, bf16[512,512]{1,0:T(8,128)(2,1)S(1)}) custom-call(bf16[512,512]{1,0:T(8,128)(2,1)} %q_hbm.1, bf16[512,512]{1,0:T(8,128)(2,1)} %k_hbm.1, bf16[512,512]{1,0:T(8,128)(2,1)} %v_hbm.1, bf16[512,512]{1,0:T(8,128)(2,1)} %g_hbm.1, ...), custom_call_target="tpu_custom_call" | custom-call | tf_op jit(solution)/shard_map/attention/pallas_call | solution.py:333
  55.8 1.3 %store.1 = (bf16[512,512]{1,0:T(8,128)(2,1)}, bf16[512,512]{1,0:T(8,128)(2,1)}, bf16[512,512]{1,0:T(8,128)(2,1)}, bf16[512,512]{1,0:T(8,128)(2,1)}) custom-call(bf16[512,512]{1,0:T(8,128)(2,1)S(1)} %get-tuple-element.8.refs_0_, bf16[512,512]{1,0:T(8,128)(2,1)S(1)} %get-tuple-element.9.refs_1_, bf16[512,512]{1,0:T(8,128)(2,1)S(1)} %get-tuple-element.10.refs_2_, ...), custom_call_target="tpu_custom_call" | custom-call | tf_op jit(solution)/shard_map/store/pallas_call | solution.py:367

commit v4 on v3

--- a/solution.py
+++ b/solution.py
@@ -244,7 +244,7 @@
         for r in range(4):
             packed = jnp.where(row == first + r, by_token[:, r * HD : (r + 1) * HD], packed)
     sums_out[...] = packed
-    for other in others(lane, n_head):
+    for other in reversed(others(lane, n_head)):
         pltpu.make_async_remote_copy(
             src_ref=sums_out, dst_ref=sums.at[lane], send_sem=sums_send, recv_sem=sums_recv,
             device_id=along_head(other), device_id_type=MESH,
@@ -282,13 +282,6 @@
         state = prior[pl.ds(h * SPLIT, SPLIT)].reshape(HD, HD)
         query_grad_ref[:, columns_of(h)] = (inner + by_state_transposed(do[h], state)).astype(BF16)
 
-    @functools.partial(each, HEADS_HERE)
-    def key_products(h):
-        for at in range(SPLIT):
-            give_totals(1, h * SPLIT + at)
-        inner_key[h] = sum_after(v[h], do[h], q[h], above)
-        inner_value[h] = sum_after(k[h], q[h], do[h], above)
-
     sums_wait.wait_send()
 
     @functools.partial(each, GROUPS)
@@ -296,9 +289,27 @@
         wait_sent(0, group, parts.at[0], NZ - 1)
         wait_sent(1, group, totals.at[0], n_y - 1)
         wait_sent(2, group, prior, NZ - 1)
+
+    def key_products(h):
+        inner_key[h] = sum_after(v[h], do[h], q[h], above)
+        inner_value[h] = sum_after(k[h], q[h], do[h], above)
+
+    @functools.partial(each, HEADS_HERE)
+    def totals_and_products(h):
+        for at in range(SPLIT):
+            give_totals(1, h * SPLIT + at)
+
+        @pl.when(h < HEADS_HERE - 1)
+        def products():
+            key_products(h)
+
+    each(GROUPS, lambda group: give_prefixes(1, group, later))
+    each(1, lambda h: key_products(h + HEADS_HERE - 1))
+
+    @functools.partial(each, GROUPS)
+    def middle_sends(group):
         wait_sent(3, group, parts.at[1], NZ - 1)
-
-    each(GROUPS, lambda group: give_prefixes(1, group, later))
+        wait_sent(4, group, totals.at[1], n_y - 1)
 
     @functools.partial(each, HEADS_HERE)
     def key_and_value_grads(h):
@@ -308,7 +319,6 @@
 
     @functools.partial(each, GROUPS)
     def last_sends(group):
-        wait_sent(4, group, totals.at[1], n_y - 1)
         wait_sent(5, group, later, NZ - 1)
 
 

time: 57.3 us -> 57.3 us (level); the launches traced: 57.2 us -> 56.1 us
  Pallas kernels: 56.5 us -> 55.5 us
    pallas_call x1, Pallas kernels: 55.2 us -> 54.2 us  [shards(): pl.pallas_call(functools.partial(attention_kernel, n_y, n_head), out_shap...]
where the time goes in v4:
time: 57.3 us; the launch traced here: 56.1 us
  Pallas kernels  55.5 us (97%)
  between operations  0.64 us (1%)
    pallas_call x1, Pallas kernels, shards(): pl.pallas_call(functools.partial(attention_kernel, n_y, n_head), out_shap...  54.2 us
    pallas_call x1, Pallas kernels, shards(): pl.pallas_call(store_kernel, out_shape=[whole] * 4, in_specs=[anywhere] *...  1.35 us

profile of v4, /device:TPU:1, one launch (start us, length us, event | category | flops | bytes accessed | tf_op | source)
XLA Modules:
  0.0 56.1 jit_solution(4359000901516449523)
XLA Ops:
  0.6 54.2 %attention.1 = (bf16[512,512]{1,0:T(8,128)(2,1)S(1)}, bf16[512,512]{1,0:T(8,128)(2,1)S(1)}, bf16[512,512]{1,0:T(8,128)(2,1)S(1)}, bf16[512,512]{1,0:T(8,128)(2,1)S(1)}) custom-call(bf16[512,512]{1,0:T(8,128)(2,1)} %q_hbm.1, bf16[512,512]{1,0:T(8,128)(2,1)} %k_hbm.1, bf16[512,512]{1,0:T(8,128)(2,1)} %v_hbm.1, bf16[512,512]{1,0:T(8,128)(2,1)} %g_hbm.1, ...), custom_call_target="tpu_custom_call" | custom-call | tf_op jit(solution)/shard_map/attention/pallas_call | solution.py:343
  54.8 1.3 %store.1 = (bf16[512,512]{1,0:T(8,128)(2,1)}, bf16[512,512]{1,0:T(8,128)(2,1)}, bf16[512,512]{1,0:T(8,128)(2,1)}, bf16[512,512]{1,0:T(8,128)(2,1)}) custom-call(bf16[512,512]{1,0:T(8,128)(2,1)S(1)} %get-tuple-element.8.refs_0_, bf16[512,512]{1,0:T(8,128)(2,1)S(1)} %get-tuple-element.9.refs_1_, bf16[512,512]{1,0:T(8,128)(2,1)S(1)} %get-tuple-element.10.refs_2_, ...), custom_call_target="tpu_custom_call" | custom-call | tf_op jit(solution)/shard_map/store/pallas_call | solution.py:377
